TPU v7x, 32 devices: a whole 2x2x4 slice. The times are simulated.
32 devices in a mesh: groups: 2 (over x), cell: 16 (over z, y, core).
Axes of the slice: x: 2, y: 2, z: 4, core: 2. Of those that a mesh axis runs over, the one named last changes fastest.
Arguments:
- frames: bfloat16 [4096, 8, 512], P(('groups', 'cell')), parts along dimension 0
- norm_time: float32 [512], replicated, may hold values from 0.1 to 1.9
- t_wq: bfloat16 [512, 512], replicated
- t_wkv: bfloat16 [512, 1024], replicated
- t_wo: bfloat16 [512, 512], replicated, may hold values from -0.25 to 0.25
- norm_space: float32 [512], replicated, may hold values from 0.1 to 1.9
- s_wq: bfloat16 [512, 512], replicated
- s_wkv: bfloat16 [512, 1024], replicated
- s_wo: bfloat16 [512, 512], replicated, may hold values from -0.25 to 0.25
- norm_mlp: float32 [512], replicated, may hold values from 0.1 to 1.9
- w_gate: bfloat16 [512, 2048], replicated, may hold values from -0.25 to 0.25
- w_up: bfloat16 [512, 2048], replicated, may hold values from -0.25 to 0.25
- w_down: bfloat16 [2048, 512], replicated, may hold values from -0.125 to 0.125
- nbr_blocks: int32 [32, 3], P(('groups', 'cell')), parts along dimension 0, may hold values from 0 to 15, as said below
- nbr_count: int32 [32], P(('groups', 'cell')), parts along dimension 0, may hold values from 1 to 3, as said below
Outputs:
- forecast_rows: bfloat16 [4096, 8, 512], P(('groups', 'cell')), parts along dimension 0
There are 2 independent parts, one for each index of `groups`. A program takes and returns all parts, laid end to end along the dimension named above; an argument that names none is the same for every part. Nothing has to cross between parts.
Inputs may be any that keep to these rules, and one draw needn't show every extreme that they name: `nbr_blocks`: row b lists distinct blocks b + o modulo 16 with 1 <= |o| <= 2; only the first nbr_count[b] entries of a row are used, the others are such blocks too. Block 0 lists block 15 and block 1 lists block 0, each as its first entry. `nbr_count`: some block uses all 3 entries and some block uses one.
All inputs are finite; a program needn't handle non-finite values.
Results may differ from a plain program's by a relative error of at most 0.018.
Values may be sent and summed in bfloat16 or wider, within the bound.
A program may use at most 128 MiB of HBM per device.

v0:
```python
import functools
import math

import jax
import jax.numpy as jnp
from jax import lax
from jax.experimental import pallas as pl
from jax.experimental.pallas import tpu as pltpu
from jax.sharding import PartitionSpec as P

HEADS = 8
HEAD_DIM = 64
BLOCK = 128
NBR_MAX = 3
EPS = 1e-05
LANES = 128
NEG = -1e30
MESH = pl.DeviceIdType.MESH
F32 = jnp.float32
BF16 = jnp.bfloat16

GROUPS = 4
CHUNKS = 4


def norm(rows, gain):
    scaled = rows * lax.rsqrt(jnp.mean(rows * rows, axis=-1, keepdims=True) + EPS)
    return (scaled * gain).astype(BF16)


def dot(a, b):
    return jnp.dot(a, b, preferred_element_type=F32)


def dot_t(a, b):
    return lax.dot_general(a, b, (((1,), (1,)), ((), ())), preferred_element_type=F32)


def paired(query):
    low = lax.broadcasted_iota(jnp.int32, query.shape, 1) < HEAD_DIM
    zero = jnp.zeros_like(query)
    return jnp.concatenate([jnp.where(low, query, zero), jnp.where(low, zero, query)], axis=0)


def attend(query, keys, values, bias):
    rows = query.shape[0]
    scores = dot_t(paired(query), keys) + bias
    top = jnp.max(scores, axis=-1, keepdims=True)
    weights = jnp.exp(scores - top)
    total = jnp.sum(weights, axis=-1, keepdims=True)
    context = dot(weights.astype(BF16), values) / total
    low = lax.broadcasted_iota(jnp.int32, (rows, LANES), 1) < HEAD_DIM
    return jnp.where(low, context[:rows], context[rows:]).astype(BF16)


def layer(
    n, steps,
    nbr, cnt, g_time, g_space, g_mlp, frames,
    h_twq, h_twkv, h_two, h_swq, h_swkv, h_swo, h_gate, h_up, h_down,
    out,
    land, mixed, win, q, kv, ctx, outf,
    twq, twkv, two, swq, swkv, swo, gate, up, down,
    w_sem, own_sem, a_send, a_recv, n_send, n_recv,
):
    me = lax.axis_index("cell")
    width = frames.shape[-1]
    parts = width // LANES
    rows = land.shape[0] * land.shape[1]
    group_rows = rows // GROUPS
    per_group = n // GROUPS
    group_cells = group_rows // steps
    per_chunk = steps // CHUNKS
    own = 4 * BLOCK
    scale = 1.0 / math.sqrt(HEAD_DIM)

    weights = [
        pltpu.make_async_copy(src, dst, w_sem.at[i])
        for i, (src, dst) in enumerate(
            [(h_twq, twq), (h_twkv, twkv), (h_two, two), (h_swq, swq), (h_swkv, swkv),
             (h_swo, swo), (h_gate, gate), (h_up, up), (h_down, down)]
        )
    ]
    for copy in weights[:3]:
        copy.start()
    own_copy = pltpu.make_async_copy(frames.at[me], land.at[me], own_sem)
    own_copy.start()

    barrier = pltpu.get_barrier_semaphore()

    def greet(d, carry):
        pl.semaphore_signal(
            barrier, inc=1, device_id={"cell": lax.rem(me + d, n)}, device_id_type=MESH
        )
        return carry

    lax.fori_loop(1, n, greet, 0)
    pl.semaphore_wait(barrier, n - 1)

    def to_peer(d):
        dest = lax.rem(me + d, n)
        return pltpu.make_async_remote_copy(
            src_ref=frames.at[dest], dst_ref=land.at[me],
            send_sem=a_send.at[d], recv_sem=a_recv.at[d],
            device_id={"cell": dest}, device_id_type=MESH,
        )

    def send(d, carry):
        to_peer(d).start()
        return carry

    lax.fori_loop(1, n, send, 0)
    for copy in weights[3:]:
        copy.start()
    for copy in weights[:3]:
        copy.wait()
    own_copy.wait()

    first = me // per_group
    r = lax.broadcasted_iota(jnp.int32, (2 * LANES, LANES), 0) % LANES
    c = lax.broadcasted_iota(jnp.int32, (2 * LANES, LANES), 1)
    causal = jnp.where((r // steps == c // steps) & (r >= c), 0.0, NEG).astype(F32)

    def temporal(s, carry):
        g = lax.rem(first + s, GROUPS)

        def arrive(k, inner):
            src = g * per_group + k
            d = lax.rem(me - src + n, n)

            @pl.when(src != me)
            def _():
                pltpu.make_async_remote_copy(
                    src_ref=frames.at[src], dst_ref=land.at[src],
                    send_sem=a_send.at[d], recv_sem=a_recv.at[d],
                    device_id={"cell": src}, device_id_type=MESH,
                ).wait_recv()

            return inner

        lax.fori_loop(0, per_group, arrive, 0)
        x = land[pl.ds(g * per_group, per_group)].reshape(group_rows, width).astype(F32)
        normed = norm(x, g_time[...])
        tq = (dot(normed, twq[...]) * scale).astype(BF16)
        tkv = dot(normed, twkv[...]).astype(BF16)
        blocks = []
        for b in range(group_rows // LANES):
            part = slice(b * LANES, (b + 1) * LANES)
            heads = [
                attend(
                    tq[part, p * LANES : (p + 1) * LANES],
                    tkv[part, p * LANES : (p + 1) * LANES],
                    tkv[part, width + p * LANES : width + (p + 1) * LANES],
                    causal,
                )
                for p in range(parts)
            ]
            blocks.append(jnp.concatenate(heads, axis=1))
        tctx = jnp.concatenate(blocks, axis=0)
        mix = (x + dot(tctx, two[...])).astype(BF16).astype(F32)
        at = pl.multiple_of(g * group_rows, group_rows)
        for p in range(parts):
            mixed[p, pl.ds(at, group_rows), :] = mix[:, p * LANES : (p + 1) * LANES]
        cell = pl.multiple_of(own + g * group_cells, group_cells)
        for t in range(steps):
            sp = jnp.concatenate(
                [mixed[p, pl.ds(at + t, group_cells, stride=steps), :] for p in range(parts)],
                axis=1,
            )
            win[t, pl.ds(cell, group_cells), :] = norm(sp, g_space[...])
        return carry

    lax.fori_loop(0, GROUPS, temporal, 0)

    core = lax.rem(me, 2)
    side = lax.rem(me // 2, 2)
    mate = me + 1 - 2 * core
    across = me + 2 - 4 * side
    onward = lax.rem(me + n + 4 - 8 * side, n)
    last_slot = lax.rem(core + side, 2)

    def hop(kind, j, src, dst, dest):
        at = pl.ds(j * per_chunk, per_chunk)
        return pltpu.make_async_remote_copy(
            src_ref=win.at[at, pl.ds(pl.multiple_of(src * BLOCK, BLOCK), BLOCK)],
            dst_ref=win.at[at, pl.ds(dst * BLOCK, BLOCK)],
            send_sem=n_send.at[kind, j], recv_sem=n_recv.at[kind, j],
            device_id={"cell": dest}, device_id_type=MESH,
        )

    def hop_across(j):
        return hop(0, j, 4, 0, across)

    def hop_onward(j):
        return hop(1, j, 0, 1, onward)

    def hop_mate(j):
        return hop(2, j, 4, 2, mate)

    def hop_last(j):
        return hop(3, j, last_slot, 3, mate)

    def send_own(j, carry):
        hop_across(j).start()
        hop_mate(j).start()
        return carry

    lax.fori_loop(0, CHUNKS, send_own, 0)
    for copy in weights[3:]:
        copy.wait()

    def own_pairs(j, carry):
        t = j * per_chunk
        sn = win[pl.ds(t, per_chunk), pl.ds(own, BLOCK), :].reshape(per_chunk * BLOCK, width)
        q[pl.ds(t, per_chunk)] = (
            (dot(sn, swq[...]) * scale).astype(BF16).reshape(per_chunk, BLOCK, width)
        )
        kv[pl.ds(t, per_chunk), pl.ds(own, BLOCK), :] = (
            dot(sn, swkv[...]).astype(BF16).reshape(per_chunk, BLOCK, 2 * width)
        )
        return carry

    lax.fori_loop(0, CHUNKS, own_pairs, 0)

    for j in range(2):
        hop_across(j).wait_recv()
        hop_onward(j).start()
    hop_onward(0).wait_recv()
    hop_last(0).start()

    chip = me // 2
    adjacent = lax.rem(chip + n // 2 - 1 + 2 * side, n // 2)
    ids = [across, 2 * adjacent + core, mate, lax.rem(me + n - 1 + 2 * core, n)]
    biases = []
    for block in ids:
        hit = jnp.int32(0)
        for j in range(NBR_MAX):
            hit = hit + jnp.where((nbr[0, j] == block) & (j < cnt[0]), 1, 0)
        biases.append(jnp.full((1, BLOCK), jnp.where(hit > 0, 0.0, NEG), F32))
    biases.append(jnp.zeros((1, BLOCK), F32))
    bias = jnp.concatenate(biases, axis=1)

    def chunk(j, carry):
        hop_mate(j).wait_recv()
        hop_last(j).wait_recv()

        def spatial(k, inner):
            t = j * per_chunk + k
            kv[t, pl.ds(0, own), :] = dot(win[t, pl.ds(0, own), :], swkv[...]).astype(BF16)
            for p in range(parts):
                lanes = slice(p * LANES, (p + 1) * LANES)
                ctx[k, :, lanes] = attend(
                    q[t, :, lanes], kv[t, :, lanes],
                    kv[t, :, width + p * LANES : width + (p + 1) * LANES], bias,
                )
            return inner

        lax.fori_loop(0, per_chunk, spatial, 0)

        @pl.when(j + 2 < CHUNKS)
        def _():
            hop_across(j + 2).wait_recv()
            hop_onward(j + 2).start()

        @pl.when(j + 1 < CHUNKS)
        def _():
            hop_onward(j + 1).wait_recv()
            hop_last(j + 1).start()

        spaced = jnp.concatenate(
            [
                jnp.concatenate(
                    [mixed[p, pl.ds(j * per_chunk + k, BLOCK, stride=steps), :] for p in range(parts)],
                    axis=1,
                )
                for k in range(per_chunk)
            ],
            axis=0,
        )
        after = (spaced + dot(ctx[...].reshape(per_chunk * BLOCK, width), swo[...])).astype(BF16)
        after = after.astype(F32)
        mn = norm(after, g_mlp[...])
        total = after
        hidden_width = gate.shape[1]
        piece = min(512, hidden_width)
        for f in range(0, hidden_width, piece):
            v = dot(mn, gate[:, f : f + piece])
            u = dot(mn, up[:, f : f + piece])
            hidden = (v / (1.0 + jnp.exp(-v)) * u).astype(BF16)
            total = total + dot(hidden, down[f : f + piece, :])
        for k in range(per_chunk):
            for p in range(parts):
                outf[p, pl.ds(j * per_chunk + k, BLOCK, stride=steps), :] = total[
                    k * BLOCK : (k + 1) * BLOCK, p * LANES : (p + 1) * LANES
                ]
        return carry

    lax.fori_loop(0, CHUNKS, chunk, 0)

    for p in range(parts):
        out[:, p * LANES : (p + 1) * LANES] = outf[p].astype(BF16)

    def drain(d, carry):
        to_peer(d).wait_send()
        return carry

    lax.fori_loop(1, n, drain, 0)

    def drain_hops(j, carry):
        hop_across(j).wait_send()
        hop_onward(j).wait_send()
        hop_mate(j).wait_send()
        hop_last(j).wait_send()
        return carry

    lax.fori_loop(0, CHUNKS, drain_hops, 0)


def per_device(
    frames, norm_time, t_wq, t_wkv, t_wo, norm_space, s_wq, s_wkv, s_wo, norm_mlp,
    w_gate, w_up, w_down, nbr_blocks, nbr_count,
):
    n = lax.axis_size("cell")
    cells, steps, width = frames.shape
    rows = cells * steps
    hidden = w_gate.shape[1]
    parts = width // LANES
    smem = pl.BlockSpec(memory_space=pltpu.SMEM)
    vmem = pl.BlockSpec(memory_space=pltpu.VMEM)
    anyw = pl.BlockSpec(memory_space=pl.ANY)
    weights = [t_wq, t_wkv, t_wo, s_wq, s_wkv, s_wo, w_gate, w_up, w_down]
    out = pl.pallas_call(
        functools.partial(layer, n, steps),
        out_shape=jax.ShapeDtypeStruct((rows, width), BF16),
        in_specs=[smem, smem, vmem, vmem, vmem, anyw] + [anyw] * len(weights),
        out_specs=vmem,
        scratch_shapes=[
            pltpu.VMEM((n, rows // n, width), BF16),
            pltpu.VMEM((parts, rows, LANES), F32),
            pltpu.VMEM((steps, 5 * BLOCK, width), BF16),
            pltpu.VMEM((steps, BLOCK, width), BF16),
            pltpu.VMEM((steps, 5 * BLOCK, 2 * width), BF16),
            pltpu.VMEM((steps // CHUNKS, BLOCK, width), BF16),
            pltpu.VMEM((parts, rows, LANES), F32),
        ]
        + [pltpu.VMEM(w.shape, BF16) for w in weights]
        + [
            pltpu.SemaphoreType.DMA((len(weights),)),
            pltpu.SemaphoreType.DMA,
            pltpu.SemaphoreType.DMA((n,)),
            pltpu.SemaphoreType.DMA((n,)),
            pltpu.SemaphoreType.DMA((4, CHUNKS)),
            pltpu.SemaphoreType.DMA((4, CHUNKS)),
        ],
        compiler_params=pltpu.CompilerParams(
            collective_id=0, has_side_effects=True, vmem_limit_bytes=56 * 1024 * 1024
        ),
        cost_estimate=pl.CostEstimate(
            flops=2 * rows * width * (12 * width + 3 * hidden), bytes_accessed=14 * 2**20,
            transcendentals=rows * 5 * BLOCK * HEADS,
        ),
    )(
        nbr_blocks, nbr_count, norm_time[None], norm_space[None], norm_mlp[None],
        frames.reshape(n, rows // n, width), *weights,
    )
    return out.reshape(cells, steps, width)


def solution(mesh):
    split3 = P(("groups", "cell"), None, None)
    placed = (split3,) + (P(),) * 12 + (P(("groups", "cell"), None), P(("groups", "cell")))
    return jax.shard_map(
        per_device, mesh=mesh, in_specs=placed, out_specs=split3, check_vma=False
    )
```

profile of v0, /device:TPU:0, one launch (start us, length us, event | category | flops | bytes accessed | tf_op | source)
XLA Modules:
  0.0 86.3 jit_solution(14946098559273013631)
XLA Ops:
  0.7 83.4 %shard_map.145 = bf16[1024,512]{1,0:T(8,128)(2,1)} custom-call(s32[1,3]{1,0:T(1,128)} %nbr.1, s32[1]{0:T(128)S(6)} %copy.17.cnt, f32[1,512]{1,0:T(1,128)} %bitcast.7, f32[1,512]{1,0:T(1,128)} %bitcast.8, f32[1,512]{1,0:T(1,128)} %bitcast.9, bf16[16,64,512]{2,1,0:T(8,128)(2,1)} %bitcast.6, bf16[512,512]{1,0:T(8,128)(2,1)} %h_twq.1, bf16[512,1024]{1,0:T(8,128)(2,1)} %h_twkv.1, ...), custom_call_target="tpu_custom_call" | custom-call | flops 12884901888 | bytes 14680064 | tf_op jit(solution)/shard_map/pallas_call | solution.py:331
  84.0 2.3 %copy.18 = bf16[128,8,512]{2,1,0:T(8,128)(2,1)} copy(bf16[128,8,512]{2,1,0:T(8,128)(2,1)} %bitcast.5) | data formatting | bytes 2097152
where the time goes:
time: 86.7 us; the launch traced here: 86.3 us
  Pallas kernels  83.4 us (96%)
  local copies, waits for them, and re-layouts  2.26 us (3%)
    pallas_call x1, Pallas kernels, per_device(): pl.pallas_call(functools.partial(layer, n, steps), out_shape=jax.ShapeDty...  83.4 us
    unnamed x1, local copies, waits for them, and re-layouts  2.26 us

commit v1 on v0

--- a/solution.py
+++ b/solution.py
@@ -60,18 +60,28 @@
     out,
     land, mixed, win, q, kv, ctx, outf,
     twq, twkv, two, swq, swkv, swo, gate, up, down,
-    w_sem, own_sem, a_send, a_recv, n_send, n_recv,
+    w_sem, own_sem, a_send, a_recv, f_send, f_recv, n_send, n_recv,
 ):
     me = lax.axis_index("cell")
     width = frames.shape[-1]
     parts = width // LANES
-    rows = land.shape[0] * land.shape[1]
+    planes = n // 4
+    half = n // 2
+    rows = mixed.shape[2]
     group_rows = rows // GROUPS
-    per_group = n // GROUPS
+    per_group = planes // GROUPS
     group_cells = group_rows // steps
     per_chunk = steps // CHUNKS
+    got = 3 * BLOCK
     own = 4 * BLOCK
     scale = 1.0 / math.sqrt(HEAD_DIM)
+
+    plane = me // 4
+    side = lax.rem(me // 2, 2)
+    core = lax.rem(me, 2)
+    spot = 2 * plane + core
+    across = me + 2 - 4 * side
+    mate = me + 1 - 2 * core
 
     weights = [
         pltpu.make_async_copy(src, dst, w_sem.at[i])
@@ -82,68 +92,94 @@
     ]
     for copy in weights[:3]:
         copy.start()
-    own_copy = pltpu.make_async_copy(frames.at[me], land.at[me], own_sem)
+    own_copy = pltpu.make_async_copy(
+        frames.at[plane, :, core], land.at[:, plane, side, core], own_sem
+    )
     own_copy.start()
 
+    def same_side(at):
+        return 4 * (at // 2) + 2 * side + lax.rem(at, 2)
+
     barrier = pltpu.get_barrier_semaphore()
 
     def greet(d, carry):
-        pl.semaphore_signal(
-            barrier, inc=1, device_id={"cell": lax.rem(me + d, n)}, device_id_type=MESH
-        )
-        return carry
-
-    lax.fori_loop(1, n, greet, 0)
-    pl.semaphore_wait(barrier, n - 1)
+        peer = same_side(lax.rem(spot + d, half))
+        pl.semaphore_signal(barrier, inc=1, device_id={"cell": peer}, device_id_type=MESH)
+        return carry
+
+    lax.fori_loop(1, half, greet, 0)
+    pl.semaphore_signal(barrier, inc=1, device_id={"cell": across}, device_id_type=MESH)
+    pl.semaphore_wait(barrier, half)
 
     def to_peer(d):
-        dest = lax.rem(me + d, n)
+        at = lax.rem(spot + d, half)
         return pltpu.make_async_remote_copy(
-            src_ref=frames.at[dest], dst_ref=land.at[me],
+            src_ref=frames.at[at // 2, :, lax.rem(at, 2)],
+            dst_ref=land.at[:, plane, side, core],
             send_sem=a_send.at[d], recv_sem=a_recv.at[d],
-            device_id={"cell": dest}, device_id_type=MESH,
+            device_id={"cell": same_side(at)}, device_id_type=MESH,
         )
 
     def send(d, carry):
         to_peer(d).start()
         return carry
 
-    lax.fori_loop(1, n, send, 0)
+    lax.fori_loop(1, half, send, 0)
     for copy in weights[3:]:
         copy.start()
     for copy in weights[:3]:
         copy.wait()
     own_copy.wait()
 
-    first = me // per_group
+    first = plane // per_group
     r = lax.broadcasted_iota(jnp.int32, (2 * LANES, LANES), 0) % LANES
     c = lax.broadcasted_iota(jnp.int32, (2 * LANES, LANES), 1)
     causal = jnp.where((r // steps == c // steps) & (r >= c), 0.0, NEG).astype(F32)
 
-    def temporal(s, carry):
-        g = lax.rem(first + s, GROUPS)
-
-        def arrive(k, inner):
-            src = g * per_group + k
-            d = lax.rem(me - src + n, n)
-
-            @pl.when(src != me)
+    def group_at(e):
+        return lax.rem(first - e + GROUPS, GROUPS)
+
+    def pass_across(e):
+        block = land.at[:, pl.ds(group_at(e) * per_group, per_group), side]
+        return pltpu.make_async_remote_copy(
+            src_ref=block, dst_ref=block, send_sem=f_send.at[e], recv_sem=f_recv.at[e],
+            device_id={"cell": across}, device_id_type=MESH,
+        )
+
+    def arrive(e):
+        def one(i, inner):
+            at = group_at(e) * 2 * per_group + i
+
+            @pl.when(at != spot)
             def _():
+                d = lax.rem(spot - at + half, half)
                 pltpu.make_async_remote_copy(
-                    src_ref=frames.at[src], dst_ref=land.at[src],
+                    src_ref=frames.at[0, :, 0], dst_ref=land.at[:, at // 2, side, lax.rem(at, 2)],
                     send_sem=a_send.at[d], recv_sem=a_recv.at[d],
-                    device_id={"cell": src}, device_id_type=MESH,
+                    device_id={"cell": same_side(at)}, device_id_type=MESH,
                 ).wait_recv()
 
             return inner
 
-        lax.fori_loop(0, per_group, arrive, 0)
-        x = land[pl.ds(g * per_group, per_group)].reshape(group_rows, width).astype(F32)
+        lax.fori_loop(0, 2 * per_group, one, 0)
+        pass_across(e).start()
+
+    arrive(0)
+
+    def temporal(e, carry):
+        g = group_at(e)
+
+        @pl.when(e + 1 < GROUPS)
+        def _():
+            arrive(e + 1)
+
+        pass_across(e).wait_recv()
+        x = land[:, pl.ds(g * per_group, per_group)].reshape(2 * group_rows, width).astype(F32)
         normed = norm(x, g_time[...])
         tq = (dot(normed, twq[...]) * scale).astype(BF16)
         tkv = dot(normed, twkv[...]).astype(BF16)
         blocks = []
-        for b in range(group_rows // LANES):
+        for b in range(2 * group_rows // LANES):
             part = slice(b * LANES, (b + 1) * LANES)
             heads = [
                 attend(
@@ -158,25 +194,29 @@
         tctx = jnp.concatenate(blocks, axis=0)
         mix = (x + dot(tctx, two[...])).astype(BF16).astype(F32)
         at = pl.multiple_of(g * group_rows, group_rows)
-        for p in range(parts):
-            mixed[p, pl.ds(at, group_rows), :] = mix[:, p * LANES : (p + 1) * LANES]
-        cell = pl.multiple_of(own + g * group_cells, group_cells)
-        for t in range(steps):
-            sp = jnp.concatenate(
-                [mixed[p, pl.ds(at + t, group_cells, stride=steps), :] for p in range(parts)],
-                axis=1,
-            )
-            win[t, pl.ds(cell, group_cells), :] = norm(sp, g_space[...])
+        for b in range(2):
+            for p in range(parts):
+                mixed[b, p, pl.ds(at, group_rows), :] = mix[
+                    b * group_rows : (b + 1) * group_rows, p * LANES : (p + 1) * LANES
+                ]
+            slot = jnp.where(side == b, 4, 3)
+            cell = pl.multiple_of(slot * BLOCK + g * group_cells, group_cells)
+            for t in range(steps):
+                sp = jnp.concatenate(
+                    [
+                        mixed[b, p, pl.ds(at + t, group_cells, stride=steps), :]
+                        for p in range(parts)
+                    ],
+                    axis=1,
+                )
+                win[t, pl.ds(cell, group_cells), :] = norm(sp, g_space[...])
         return carry
 
     lax.fori_loop(0, GROUPS, temporal, 0)
 
-    core = lax.rem(me, 2)
-    side = lax.rem(me // 2, 2)
-    mate = me + 1 - 2 * core
-    across = me + 2 - 4 * side
     onward = lax.rem(me + n + 4 - 8 * side, n)
-    last_slot = lax.rem(core + side, 2)
+    has_last = core == side
+    last_slot = jnp.where(has_last, 3, 0)
 
     def hop(kind, j, src, dst, dest):
         at = pl.ds(j * per_chunk, per_chunk)
@@ -187,22 +227,31 @@
             device_id={"cell": dest}, device_id_type=MESH,
         )
 
-    def hop_across(j):
-        return hop(0, j, 4, 0, across)
-
     def hop_onward(j):
-        return hop(1, j, 0, 1, onward)
+        return hop(0, j, 3, 0, onward)
 
     def hop_mate(j):
-        return hop(2, j, 4, 2, mate)
+        return hop(1, j, 4, 1, mate)
 
     def hop_last(j):
-        return hop(3, j, last_slot, 3, mate)
+        return hop(2, j, last_slot, 2, mate)
 
     def send_own(j, carry):
-        hop_across(j).start()
+        hop_onward(j).start()
         hop_mate(j).start()
-        return carry
+
+        @pl.when(has_last)
+        def _():
+            hop_last(j).start()
+
+        return carry
+
+    def relay(j):
+        hop_onward(j).wait_recv()
+
+        @pl.when(jnp.logical_not(has_last))
+        def _():
+            hop_last(j).start()
 
     lax.fori_loop(0, CHUNKS, send_own, 0)
     for copy in weights[3:]:
@@ -214,22 +263,20 @@
         q[pl.ds(t, per_chunk)] = (
             (dot(sn, swq[...]) * scale).astype(BF16).reshape(per_chunk, BLOCK, width)
         )
-        kv[pl.ds(t, per_chunk), pl.ds(own, BLOCK), :] = (
-            dot(sn, swkv[...]).astype(BF16).reshape(per_chunk, BLOCK, 2 * width)
+        sn = win[pl.ds(t, per_chunk), pl.ds(got, 2 * BLOCK), :]
+        kv[pl.ds(t, per_chunk), pl.ds(got, 2 * BLOCK), :] = (
+            dot(sn.reshape(per_chunk * 2 * BLOCK, width), swkv[...])
+            .astype(BF16).reshape(per_chunk, 2 * BLOCK, 2 * width)
         )
         return carry
 
     lax.fori_loop(0, CHUNKS, own_pairs, 0)
 
-    for j in range(2):
-        hop_across(j).wait_recv()
-        hop_onward(j).start()
-    hop_onward(0).wait_recv()
-    hop_last(0).start()
+    relay(0)
 
     chip = me // 2
     adjacent = lax.rem(chip + n // 2 - 1 + 2 * side, n // 2)
-    ids = [across, 2 * adjacent + core, mate, lax.rem(me + n - 1 + 2 * core, n)]
+    ids = [2 * adjacent + core, mate, lax.rem(me + n - 1 + 2 * core, n), across]
     biases = []
     for block in ids:
         hit = jnp.int32(0)
@@ -245,7 +292,7 @@
 
         def spatial(k, inner):
             t = j * per_chunk + k
-            kv[t, pl.ds(0, own), :] = dot(win[t, pl.ds(0, own), :], swkv[...]).astype(BF16)
+            kv[t, pl.ds(0, got), :] = dot(win[t, pl.ds(0, got), :], swkv[...]).astype(BF16)
             for p in range(parts):
                 lanes = slice(p * LANES, (p + 1) * LANES)
                 ctx[k, :, lanes] = attend(
@@ -256,20 +303,17 @@
 
         lax.fori_loop(0, per_chunk, spatial, 0)
 
-        @pl.when(j + 2 < CHUNKS)
-        def _():
-            hop_across(j + 2).wait_recv()
-            hop_onward(j + 2).start()
-
         @pl.when(j + 1 < CHUNKS)
         def _():
-            hop_onward(j + 1).wait_recv()
-            hop_last(j + 1).start()
+            relay(j + 1)
 
         spaced = jnp.concatenate(
             [
                 jnp.concatenate(
-                    [mixed[p, pl.ds(j * per_chunk + k, BLOCK, stride=steps), :] for p in range(parts)],
+                    [
+                        mixed[side, p, pl.ds(j * per_chunk + k, BLOCK, stride=steps), :]
+                        for p in range(parts)
+                    ],
                     axis=1,
                 )
                 for k in range(per_chunk)
@@ -303,10 +347,15 @@
         to_peer(d).wait_send()
         return carry
 
-    lax.fori_loop(1, n, drain, 0)
+    lax.fori_loop(1, half, drain, 0)
+
+    def drain_across(e, carry):
+        pass_across(e).wait_send()
+        return carry
+
+    lax.fori_loop(0, GROUPS, drain_across, 0)
 
     def drain_hops(j, carry):
-        hop_across(j).wait_send()
         hop_onward(j).wait_send()
         hop_mate(j).wait_send()
         hop_last(j).wait_send()
@@ -334,8 +383,8 @@
         in_specs=[smem, smem, vmem, vmem, vmem, anyw] + [anyw] * len(weights),
         out_specs=vmem,
         scratch_shapes=[
-            pltpu.VMEM((n, rows // n, width), BF16),
-            pltpu.VMEM((parts, rows, LANES), F32),
+            pltpu.VMEM((2, n // 4, 2, 2, rows // n, width), BF16),
+            pltpu.VMEM((2, parts, rows, LANES), F32),
             pltpu.VMEM((steps, 5 * BLOCK, width), BF16),
             pltpu.VMEM((steps, BLOCK, width), BF16),
             pltpu.VMEM((steps, 5 * BLOCK, 2 * width), BF16),
@@ -346,10 +395,12 @@
         + [
             pltpu.SemaphoreType.DMA((len(weights),)),
             pltpu.SemaphoreType.DMA,
-            pltpu.SemaphoreType.DMA((n,)),
-            pltpu.SemaphoreType.DMA((n,)),
-            pltpu.SemaphoreType.DMA((4, CHUNKS)),
-            pltpu.SemaphoreType.DMA((4, CHUNKS)),
+            pltpu.SemaphoreType.DMA((n // 2,)),
+            pltpu.SemaphoreType.DMA((n // 2,)),
+            pltpu.SemaphoreType.DMA((GROUPS,)),
+            pltpu.SemaphoreType.DMA((GROUPS,)),
+            pltpu.SemaphoreType.DMA((3, CHUNKS)),
+            pltpu.SemaphoreType.DMA((3, CHUNKS)),
         ],
         compiler_params=pltpu.CompilerParams(
             collective_id=0, has_side_effects=True, vmem_limit_bytes=56 * 1024 * 1024
@@ -360,7 +411,7 @@
         ),
     )(
         nbr_blocks, nbr_count, norm_time[None], norm_space[None], norm_mlp[None],
-        frames.reshape(n, rows // n, width), *weights,
+        frames.reshape(n // 4, 2, 2, rows // n, width), *weights,
     )
     return out.reshape(cells, steps, width)
 

time: 86.7 us -> 88 us (1.015)
  Pallas kernels: 83.4 us -> 84.9 us
    pallas_call x1, Pallas kernels: 83.4 us -> 84.9 us  [per_device(): pl.pallas_call(functools.partial(layer, n, steps), out_shape=jax.ShapeDty...]
where the time goes in v1:
time: 88 us; the launch traced here: 87.8 us
  Pallas kernels  84.9 us (96%)
  local copies, waits for them, and re-layouts  2.26 us (3%)
    pallas_call x1, Pallas kernels, per_device(): pl.pallas_call(functools.partial(layer, n, steps), out_shape=jax.ShapeDty...  84.9 us
    unnamed x1, local copies, waits for them, and re-layouts  2.26 us

profile of v1, /device:TPU:0, one launch (start us, length us, event | category | flops | bytes accessed | tf_op | source)
XLA Modules:
  0.0 87.8 jit_solution(17190055275621963785)
XLA Ops:
  0.7 84.9 %shard_map.145 = bf16[1024,512]{1,0:T(8,128)(2,1)} custom-call(s32[1,3]{1,0:T(1,128)} %nbr.1, s32[1]{0:T(128)S(6)} %copy.17.cnt, f32[1,512]{1,0:T(1,128)} %bitcast.7, f32[1,512]{1,0:T(1,128)} %bitcast.8, f32[1,512]{1,0:T(1,128)} %bitcast.9, bf16[4,2,2,64,512]{4,3,2,1,0:T(8,128)(2,1)} %bitcast.6, bf16[512,512]{1,0:T(8,128)(2,1)} %h_twq.1, ...), custom_call_target="tpu_custom_call" | custom-call | flops 12884901888 | bytes 14680064 | tf_op jit(solution)/shard_map/pallas_call | solution.py:380
  85.5 2.3 %copy.18 = bf16[128,8,512]{2,1,0:T(8,128)(2,1)} copy(bf16[128,8,512]{2,1,0:T(8,128)(2,1)} %bitcast.5) | data formatting | bytes 2097152

commit v2 on v1

--- a/solution.py
+++ b/solution.py
@@ -46,11 +46,17 @@
     rows = query.shape[0]
     scores = dot_t(paired(query), keys) + bias
     top = jnp.max(scores, axis=-1, keepdims=True)
-    weights = jnp.exp(scores - top)
-    total = jnp.sum(weights, axis=-1, keepdims=True)
-    context = dot(weights.astype(BF16), values) / total
+    weights = jnp.exp2(scores - top)
     low = lax.broadcasted_iota(jnp.int32, (rows, LANES), 1) < HEAD_DIM
-    return jnp.where(low, context[:rows], context[rows:]).astype(BF16)
+    if values.shape[0] == LANES:
+        total = jnp.sum(weights, axis=-1, keepdims=True)
+        both = dot(weights.astype(BF16), values) * pl.reciprocal(total, approx=True)
+        return jnp.where(low, both[:rows], both[rows:]).astype(BF16)
+    ones = jnp.ones((values.shape[0], LANES), BF16)
+    both = dot(weights.astype(BF16), jnp.concatenate([values, ones], axis=1))
+    mixed = jnp.where(low, both[:rows, :LANES], both[rows:, :LANES])
+    total = jnp.where(low, both[:rows, LANES:], both[rows:, LANES:])
+    return (mixed * pl.reciprocal(total, approx=True)).astype(BF16)
 
 
 def layer(
@@ -74,7 +80,7 @@
     per_chunk = steps // CHUNKS
     got = 3 * BLOCK
     own = 4 * BLOCK
-    scale = 1.0 / math.sqrt(HEAD_DIM)
+    scale = math.log2(math.e) / math.sqrt(HEAD_DIM)
 
     plane = me // 4
     side = lax.rem(me // 2, 2)
@@ -120,24 +126,35 @@
             device_id={"cell": same_side(at)}, device_id_type=MESH,
         )
 
-    def send(d, carry):
-        to_peer(d).start()
-        return carry
-
-    lax.fori_loop(1, half, send, 0)
+    first = plane // per_group
+
+    def group_at(e):
+        low = lax.rem(lax.rem(first, 2) + lax.rem(jnp.int32(e), 2), 2)
+        return 2 * lax.rem(first // 2 + jnp.int32(e) // 2, 2) + low
+
+    def send_group(e):
+        def one(i, carry):
+            at = group_at(e) * 2 * per_group + i
+
+            @pl.when(at != spot)
+            def _():
+                to_peer(lax.rem(at - spot + half, half)).start()
+
+            return carry
+
+        lax.fori_loop(0, 2 * per_group, one, 0)
+
+    for e in (0, 2, 1):
+        send_group(e)
     for copy in weights[3:]:
         copy.start()
     for copy in weights[:3]:
         copy.wait()
     own_copy.wait()
 
-    first = plane // per_group
     r = lax.broadcasted_iota(jnp.int32, (2 * LANES, LANES), 0) % LANES
     c = lax.broadcasted_iota(jnp.int32, (2 * LANES, LANES), 1)
     causal = jnp.where((r // steps == c // steps) & (r >= c), 0.0, NEG).astype(F32)
-
-    def group_at(e):
-        return lax.rem(first - e + GROUPS, GROUPS)
 
     def pass_across(e):
         block = land.at[:, pl.ds(group_at(e) * per_group, per_group), side]
@@ -165,13 +182,15 @@
         pass_across(e).start()
 
     arrive(0)
+    arrive(1)
+    send_group(3)
 
     def temporal(e, carry):
         g = group_at(e)
 
-        @pl.when(e + 1 < GROUPS)
+        @pl.when(e + 2 < GROUPS)
         def _():
-            arrive(e + 1)
+            arrive(e + 2)
 
         pass_across(e).wait_recv()
         x = land[:, pl.ds(g * per_group, per_group)].reshape(2 * group_rows, width).astype(F32)
@@ -329,7 +348,7 @@
         for f in range(0, hidden_width, piece):
             v = dot(mn, gate[:, f : f + piece])
             u = dot(mn, up[:, f : f + piece])
-            hidden = (v / (1.0 + jnp.exp(-v)) * u).astype(BF16)
+            hidden = ((0.5 * v) * (1.0 + jnp.tanh(0.5 * v)) * u).astype(BF16)
             total = total + dot(hidden, down[f : f + piece, :])
         for k in range(per_chunk):
             for p in range(parts):

time: 88 us -> 77.7 us (0.88)
  Pallas kernels: 84.9 us -> 74.1 us
    pallas_call x1, Pallas kernels: 84.9 us -> 74.1 us  [per_device(): pl.pallas_call(functools.partial(layer, n, steps), out_shape=jax.ShapeDty...]
where the time goes in v2:
time: 77.7 us; the launch traced here: 77 us
  Pallas kernels  74.1 us (95%)
  local copies, waits for them, and re-layouts  2.26 us (3%)
    pallas_call x1, Pallas kernels, per_device(): pl.pallas_call(functools.partial(layer, n, steps), out_shape=jax.ShapeDty...  74.1 us
    unnamed x1, local copies, waits for them, and re-layouts  2.26 us

profile of v2, /device:TPU:0, one launch (start us, length us, event | category | flops | bytes accessed | tf_op | source)
XLA Modules:
  0.0 77.0 jit_solution(6874205256161819317)
XLA Ops:
  0.7 74.1 %shard_map.145 = bf16[1024,512]{1,0:T(8,128)(2,1)} custom-call(s32[1,3]{1,0:T(1,128)} %nbr.1, s32[1]{0:T(128)S(6)} %copy.17.cnt, f32[1,512]{1,0:T(1,128)} %bitcast.7, f32[1,512]{1,0:T(1,128)} %bitcast.8, f32[1,512]{1,0:T(1,128)} %bitcast.9, bf16[4,2,2,64,512]{4,3,2,1,0:T(8,128)(2,1)} %bitcast.6, bf16[512,512]{1,0:T(8,128)(2,1)} %h_twq.1, ...), custom_call_target="tpu_custom_call" | custom-call | flops 12884901888 | bytes 14680064 | tf_op jit(solution)/shard_map/pallas_call | solution.py:399
  74.8 2.3 %copy.18 = bf16[128,8,512]{2,1,0:T(8,128)(2,1)} copy(bf16[128,8,512]{2,1,0:T(8,128)(2,1)} %bitcast.5) | data formatting | bytes 2097152
